TPU v7x, 512 devices: a whole 4x8x8 slice. The times are simulated.
512 devices in a mesh: seq: 32 (over x, y), head: 16 (over z, core).
Axes of the slice: x: 4, y: 8, z: 8, core: 2. Of those that a mesh axis runs over, the one named last changes fastest.
Arguments:
- queries: bfloat16 [65536, 4096], P(('seq', 'head')), may hold values from -6 to 6
- keys: bfloat16 [65536, 4096], P(('seq', 'head')), may hold values from -6 to 6
- values: bfloat16 [65536, 4096], P(('seq', 'head')), may hold values from -400 to 400
- log_decay: bfloat16 [65536, 32], P(('seq', 'head')), may hold values from -1 to 0
- cached_state: float32 [32, 128, 128], P('head'), may hold values from -384 to 384
- norm_gain: float32 [32, 128], P('head'), may hold values from 0.25 to 1.75
Outputs:
- attended: bfloat16 [65536, 4096], P(('seq', 'head'))
- final_state: float32 [32, 128, 128], P('head', 'seq')
All inputs are finite; a program needn't handle non-finite values.
Results may differ from a plain program's by a relative error of at most 0.0035.
Values may be sent and summed in bfloat16 or wider, within the bound.
A program may use at most 64 MiB of HBM per device.

v0:
```python
import jax
import jax.numpy as jnp
from jax import lax
from jax.sharding import PartitionSpec as P

BLK = 512


def entering(x, axis, combine, identity):
    length, mine = (lax.axis_size(axis), lax.axis_index(axis))
    everything = jax.tree.map(lambda part: lax.all_gather(part, axis), x)
    start = jax.tree.map(
        lambda part, zero: jnp.broadcast_to(jnp.asarray(zero, part.dtype), part.shape), x, identity
    )

    def step(k, before):
        reached = k < mine
        new = combine(before, jax.tree.map(lambda part: part[k], everything))
        return jax.tree.map(lambda a, b: jnp.where(reached, a, b), new, before)

    return lax.fori_loop(0, length, step, start)


def broadcast(value, axis, source):
    kept = jnp.where(lax.axis_index(axis) == source, value, 0).astype(value.dtype)
    return lax.psum(kept, axis)


def combine(earlier, later):
    return (earlier[0] * later[0], later[0][:, None, None] * earlier[1] + later[1])


def local(queries, keys, values, log_decay, cached_state, norm_gain):
    query_group, key_group, value_group, decay_group = (
        lax.all_to_all(queries, "head", split_axis=1, concat_axis=0, tiled=True),
        lax.all_to_all(keys, "head", split_axis=1, concat_axis=0, tiled=True),
        lax.all_to_all(values, "head", split_axis=1, concat_axis=0, tiled=True),
        lax.all_to_all(log_decay, "head", split_axis=1, concat_axis=0, tiled=True),
    )
    length = key_group.shape[0]
    groups = decay_group.shape[1]
    head_size = key_group.shape[1] // groups
    block_count = length // BLK
    key_blocks = key_group.reshape(block_count, BLK, groups, head_size)
    value_blocks = value_group.reshape(block_count, BLK, groups, head_size)
    running = jnp.cumsum(decay_group.astype(jnp.float32).reshape(block_count, BLK, groups), axis=1)
    ending = running[:, -1, :]
    keys_scaled = key_blocks.astype(jnp.float32) * jnp.exp(ending[:, None, :] - running)[..., None]
    block_states = jnp.einsum(
        "bthd,bthe->bhde",
        keys_scaled,
        value_blocks.astype(jnp.float32),
        precision=lax.Precision.HIGHEST,
    )
    block_decay = jnp.exp(ending)

    def compose(state_pair, block_pair):
        joined = combine(state_pair, block_pair)
        return (joined, state_pair)

    unit_decay = jnp.ones((groups,), jnp.float32)
    empty_state = jnp.zeros((groups, head_size, head_size), jnp.float32)
    (device_decay, device_state), (start_decay, start_state) = lax.scan(
        compose, (unit_decay, empty_state), (block_decay, block_states)
    )
    prior_decay, prior_state = entering(
        (device_decay, device_state), "seq", combine, (unit_decay, empty_state)
    )
    entry_state = prior_decay[:, None, None] * cached_state + prior_state
    leaving = device_decay[:, None, None] * entry_state + device_state
    whole_final = broadcast(leaving, "seq", lax.axis_size("seq") - 1)
    share_rows = head_size // lax.axis_size("seq")
    final_state = lax.dynamic_slice_in_dim(
        whole_final, lax.axis_index("seq") * share_rows, share_rows, 1
    )
    query_blocks = query_group.reshape(block_count, BLK, groups, head_size)
    starts = start_decay[:, :, None, None] * entry_state[None] + start_state
    carried = jnp.einsum(
        "bthd,bhde->bthe", query_blocks.astype(jnp.float32), starts, precision=lax.Precision.HIGHEST
    )
    carried = carried * jnp.exp(running)[..., None]
    scores = jnp.einsum(
        "bthd,bshd->bhts", query_blocks, key_blocks, preferred_element_type=jnp.float32
    )
    across = jnp.transpose(running, (0, 2, 1))
    log_gaps = across[:, :, :, None] - across[:, :, None, :]
    positions = jnp.arange(BLK, dtype=jnp.int32)
    causal = (positions[:, None] >= positions[None, :])[None, None]
    decay_mask = jnp.where(causal, jnp.exp(jnp.where(causal, log_gaps, 0.0)), 0.0)
    weights = (scores * decay_mask).astype(jnp.bfloat16)
    within = jnp.einsum(
        "bhts,bshd->bthd", weights, value_blocks, preferred_element_type=jnp.float32
    )
    mixed_out = within + carried
    scale_rows = lax.rsqrt(jnp.mean(mixed_out * mixed_out, axis=-1, keepdims=True) + 1e-06)
    normed = mixed_out * scale_rows * norm_gain[None, None]
    rounded = normed.astype(jnp.bfloat16).reshape(length, groups * head_size)
    attended = lax.all_to_all(rounded, "head", split_axis=0, concat_axis=1, tiled=True)
    return (attended, final_state)


def solution(mesh):
    placed = (
        P(("seq", "head"), None),
        P(("seq", "head"), None),
        P(("seq", "head"), None),
        P(("seq", "head"), None),
        P("head", None, None),
        P("head", None),
    )
    return jax.shard_map(
        local,
        mesh=mesh,
        in_specs=placed,
        out_specs=(P(("seq", "head"), None), P("head", "seq", None)),
        check_vma=False,
    )
```

profile of v0, /device:TPU:1, one launch (start us, length us, event | category | flops | bytes accessed | tf_op | source)
XLA Modules:
  0.0 444.7 jit_solution(17994706608042003626)
XLA Ops:
  7.2 11.8 %all-to-all-start.2 = ((bf16[128,16,2]{0,2,1:T(2,128)(2,1)}), bf16[128,16,2]{0,2,1:T(2,128)(2,1)S(1)}, u32[]{:S(2)}, u32[]{:S(2)}) async-start(bf16[128,16,2]{0,2,1:T(2,128)(2,1)} %bitcast.73), calls=%async_computation.2 | async-start | bytes 16384 | tf_op jit(solution)/shard_map/all_to_all | solution.py:38
  19.0 2.4 copy.129
  21.4 4.5 %all-to-all-done.2 = bf16[128,16,2]{0,2,1:T(2,128)(2,1)S(1)} async-done(((bf16[128,16,2]{0,2,1:T(2,128)(2,1)}), bf16[128,16,2]{0,2,1:T(2,128)(2,1)S(1)}, u32[]{:S(2)}, u32[]{:S(2)}) %all-to-all-start.2) | async-done | bytes 8224 | tf_op jit(solution)/shard_map/all_to_all | solution.py:38
  25.9 4.1 all-to-all-start.1
  31.1 26.9 %all-to-all-done.1 = bf16[128,16,256]{2,0,1:T(8,128)(2,1)S(1)} async-done(((bf16[128,16,256]{2,0,1:T(8,128)(2,1)}), bf16[128,16,256]{2,0,1:T(8,128)(2,1)S(1)}, u32[]{:S(2)}, u32[]{:S(2)}) %all-to-all-start.1) | async-done | bytes 1048608 | tf_op jit(solution)/shard_map/all_to_all | solution.py:36
  58.0 3.6 all-to-all-start.3
  61.7 2.4 reduce-window.6
  65.9 1.3 copy.89
  67.6 21.8 %all-to-all-done.3 = bf16[128,16,256]{2,0,1:T(8,128)(2,1)S(1)} async-done(((bf16[128,16,256]{2,0,1:T(8,128)(2,1)}), bf16[128,16,256]{2,0,1:T(8,128)(2,1)S(1)}, u32[]{:S(2)}, u32[]{:S(2)}) %all-to-all-start.3) | async-done | bytes 1048608 | tf_op jit(solution)/shard_map/all_to_all | solution.py:37
  89.8 4.7 %convert_multiply_fusion = f32[4,512,2,128]{3,2,1,0:T(2,128)S(1)} fusion(bf16[4,512,2,128]{3,2,1,0:T(2,128)(2,1)S(1)} %reshape.100, f32[4,512,2]{2,1,0:T(8,128)} %copy.89), kind=kLoop, calls=%fused_computation.22 | loop fusion | flops 1048576 | bytes 3162112 | tf_op jit(solution)/shard_map/mul | solution.py:48
  94.5 1.9 fusion.9
  96.4 8.2 %while.33 = (s32[]{:T(128)}, f32[2]{0:T(128)S(1)}, f32[2,128,128]{2,1,0:T(8,128)S(1)}, f32[4,2]{1,0:T(4,128)}, f32[4,2,128,128]{3,2,1,0:T(8,128)}, /*index=5*/f3...) while((s32[]{:T(128)}, f32[2]{0:T(128)S(1)}, ...), condition=%wide.region_3.4_spmd.clone, body=%wide.region_2.3_spmd.clone.sunk | while | flops 131079 | bytes 656053 | solution.py:63
  97.1 1.3 dynamic_update_slice.14
  99.2 1.3 dynamic_update_slice.14
  101.2 1.3 dynamic_update_slice.14
  105.2 2.3 copy.130
  107.5 3.6 all-to-all-start
  111.1 1.4 dynamic-slice
  113.3 1.3 copy.95
  115.2 1.4 dynamic-update-slice
  116.5 62.7 %all-reduce = f32[64]{0:T(128)} all-reduce(f32[64]{0:T(128)} %dynamic-update-slice), channel_id=2, replica_groups=mesh['seq'=32,'head'=16] {'seq'}, use_global_device_ids=true, to_apply=%add | all-reduce | flops 64 | bytes 512
  179.2 1.3 reshape.106
  181.6 6.4 %fusion.4 = f32[4,2,512,128]{2,3,1,0:T(8,128)} fusion(f32[4,2,512]{2,1,0:T(2,128)S(1)} %reshape.113, pred[512,512]{1,0:T(8,128)(4,1)S(1)} %iota_compare_fusion, bf16[4,512,2,128]{3,2,1,0:T(2,128)(2,1)S(1)} %reshape.100, bf16[4,512,2,128]{3,2,1,0:T(2,128)(2,1)S(1)} %reshape.103, bf16[4,512,2,128]{3,2,1,0:T(2,128)(2,1)} %reshape.99), kind=kOutput, calls=%fused_computation.13 | convolution fusion | flops 1084227584 | bytes 5521408 | tf_op jit(solution)/shard_map/bhts,bshd->bthd/dot_general | solution.py:91
  188.0 73.1 %while.34 = (s32[]{:T(128)}, f32[2]{0:T(128)}, f32[2,128,128]{2,1,0:T(8,128)S(1)}, s32[]{:T(128)}, f32[32,2]{1,0:T(8,128)}, /*index=5*/f32[32,2,128,128]{3,2,1,0:T(8,128)}, s32[]{:T(128)}, s32[]{:T(128)}) while((s32[]{:T(128)}, f32[2]{0:T(128)}, f32[2,128,128]{2,1,0:T(8,128)S(1)}, s32[]{:T(128)}, f32[32,2]{1,0:T(8,128)}, ...), condition=%wide.region_5.6_spmd.clone, body=%wide.region_4.5_spmd.clone.sunk | while | flops 131082 | bytes 393371 | solution.py:21
  188.0 1.3 broadcast_select_fusion.4
  261.1 1.6 add_select_fusion
  262.8 3.0 multiply_reduce_fusion
  266.9 1.5 all_to_all.71
  268.4 20.6 %all-to-all-start.4 = ((bf16[16,128,256]{2,1,0:T(8,128)(2,1)}), bf16[16,128,256]{2,1,0:T(8,128)(2,1)S(1)}, u32[]{:S(2)}, u32[]{:S(2)}) async-start(bf16[16,128,256]{2,1,0:T(8,128)(2,1)} %all_to_all.71), calls=%async_computation.4 | async-start | bytes 2097152 | tf_op jit(solution)/shard_map/all_to_all | solution.py:98
  289.7 144.9 %all-reduce.3.cloned.1.call-done = f32[2,128,128]{2,1,0:T(8,128)} async-done(((f32[2,128,128]{2,1,0:T(8,128)}), f32[2,128,128]{2,1,0:T(8,128)}) %all-reduce.3.cloned.1.call-update) | async-done | bytes 131088 | tf_op jit(solution)/shard_map/psum | solution.py:26
  434.6 1.3 constant_dynamic-slice_fusion.1
  436.5 1.3 copy.98
  (128 shorter events, 83.8 us)
Async XLA Ops:
  7.2 18.8 %all-to-all-start.2 = ((bf16[128,16,2]{0,2,1:T(2,128)(2,1)}), bf16[128,16,2]{0,2,1:T(2,128)(2,1)S(1)}, u32[]{:S(2)}, u32[]{:S(2)}) async-start(bf16[128,16,2]{0,2,1:T(2,128)(2,1)} %bitcast.73), calls=%async_computation.2 | async-start | bytes 16384 | tf_op jit(solution)/shard_map/all_to_all | solution.py:38
  19.0 11.0 %copy-start.3 = (bf16[128,4096]{1,0:T(8,128)(2,1)S(1)}, bf16[128,4096]{1,0:T(8,128)(2,1)}, u32[]{:S(2)}) copy-start(bf16[128,4096]{1,0:T(8,128)(2,1)} %param.12) | copy-start | bytes 3145732
  25.9 32.1 %all-to-all-start.1 = ((bf16[128,16,256]{2,0,1:T(8,128)(2,1)}), bf16[128,16,256]{2,0,1:T(8,128)(2,1)S(1)}, u32[]{:S(2)}, u32[]{:S(2)}) async-start(bf16[128,16,256]{2,0,1:T(8,128)(2,1)} %bitcast.51), calls=%async_computation.1 | async-start | bytes 2097152 | tf_op jit(solution)/shard_map/all_to_all | solution.py:36
  58.0 31.5 %all-to-all-start.3 = ((bf16[128,16,256]{2,0,1:T(8,128)(2,1)}), bf16[128,16,256]{2,0,1:T(8,128)(2,1)S(1)}, u32[]{:S(2)}, u32[]{:S(2)}) async-start(bf16[128,16,256]{2,0,1:T(8,128)(2,1)} %bitcast.50), calls=%async_computation.3 | async-start | bytes 2097152 | tf_op jit(solution)/shard_map/all_to_all | solution.py:37
  61.6 126.4 %all-gather.4.cloned.1.call-start = ((), (), s32[]{:S(2)}) async-start(), calls=%async_computation.6 | async-start | bytes 4325376 | tf_op jit(solution)/shard_map/all_gather | solution.py:11
  104.6 0.6 copy-start
  104.6 3.0 copy-start.6
  107.5 73.0 %all-to-all-start = ((bf16[128,16,256]{2,0,1:T(8,128)(2,1)}), bf16[128,16,256]{2,0,1:T(8,128)(2,1)S(1)}, u32[]{:S(2)}, u32[]{:S(2)}) async-start(bf16[128,16,256]{2,0,1:T(8,128)(2,1)} %bitcast.52), calls=%async_computation | async-start | bytes 2097152 | tf_op jit(solution)/shard_map/all_to_all | solution.py:35
  181.6 81.2 %copy-start.2 = (bf16[4,512,2,128]{3,2,1,0:T(2,128)(2,1)S(1)}, bf16[4,512,2,128]{3,2,1,0:T(2,128)(2,1)}, u32[]{:S(2)}) copy-start(bf16[4,512,2,128]{3,2,1,0:T(2,128)(2,1)} %reshape.99) | copy-start | bytes 3145732
  188.0 73.2 %copy-start.1 = (f32[2,128,128]{2,1,0:T(8,128)S(1)}, f32[2,128,128]{2,1,0:T(8,128)}, u32[]{:S(2)}) copy-start(f32[2,128,128]{2,1,0:T(8,128)} %copy-done) | copy-start | bytes 393220
  188.0 74.8 %copy-start.4 = (f32[4,2,128,128]{3,2,1,0:T(8,128)S(1)}, f32[4,2,128,128]{3,2,1,0:T(8,128)}, u32[]{:S(2)}) copy-start(f32[4,2,128,128]{3,2,1,0:T(8,128)} %get-tuple-element.157) | copy-start | bytes 1572868
  188.0 74.8 %copy-start.5 = (f32[4,512,2]{1,2,0:T(2,128)S(1)}, f32[4,512,2]{1,2,0:T(2,128)}, u32[]{:S(2)}) copy-start(f32[4,512,2]{1,2,0:T(2,128)} %copy.95) | copy-start | bytes 49156
  188.0 74.8 %copy-start.7 = (f32[4,2]{1,0:T(4,128)S(1)}, f32[4,2]{1,0:T(4,128)}, u32[]{:S(2)}) copy-start(f32[4,2]{1,0:T(4,128)} %get-tuple-element.152) | copy-start | bytes 100
  262.8 3.0 copy-start.8
  268.4 167.5 %all-to-all-start.4 = ((bf16[16,128,256]{2,1,0:T(8,128)(2,1)}), bf16[16,128,256]{2,1,0:T(8,128)(2,1)S(1)}, u32[]{:S(2)}, u32[]{:S(2)}) async-start(bf16[16,128,256]{2,1,0:T(8,128)(2,1)} %all_to_all.71), calls=%async_computation.4 | async-start | bytes 2097152 | tf_op jit(solution)/shard_map/all_to_all | solution.py:98
  289.0 145.6 %all-reduce.3.cloned.1.call-start = ((), (), s32[]{:S(2)}) async-start(), calls=%async_computation.5 | async-start | bytes 262144 | tf_op jit(solution)/shard_map/psum | solution.py:26
Sparse Core Ops, SparseCore 0:
  105.3 81.5 all-gather.3
  293.3 141.2 all-reduce.2
where the time goes:
time: 450 us; the launch traced here: 445 us
  waiting for transfers between devices  199 us (44%)
  other arithmetic  85.9 us (19%)
  blocking collectives  62.7 us (14%)
  starting transfers between devices  43.7 us (10%)
  local copies, waits for them, and re-layouts  26.5 us (6%)
  between operations  15 us (3%)
  matrix products  11.2 us (2%)
    psum x1, waiting for transfers between devices, broadcast(): return lax.psum(kept, axis)  145 us
    select_n x64, other arithmetic, step(): return jax.tree.map(lambda a, b: jnp.where(reached, a, b), new, before)  72.3 us
    unnamed x1, blocking collectives  62.7 us
    all_to_all x1, waiting for transfers between devices, local(): lax.all_to_all(keys, 'head', split_axis=1, concat_axis=0, tiled=True)  26.9 us
    all_to_all x1, waiting for transfers between devices, local(): lax.all_to_all(values, 'head', split_axis=1, concat_axis=0, tiled=True)  21.8 us
    all_to_all x1, starting transfers between devices, local(): lax.all_to_all(rounded, 'head', split_axis=0, concat_axis=1, tiled=True)  20.6 us
    all_to_all x1, starting transfers between devices, local(): lax.all_to_all(log_decay, 'head', split_axis=1, concat_axis=0, tiled=True)  11.8 us
  transfers between devices with their start and end apart: 7, of which 4 were waited for; matrix products, arithmetic and copies ran while one was open for 6% of the time, Pallas kernels for 0%

commit v1 on v0

v1 whole, which is shorter than its diff:
```python
import functools

import jax
import jax.numpy as jnp
from jax import lax
from jax.experimental import pallas as pl
from jax.experimental.pallas import tpu as pltpu
from jax.sharding import PartitionSpec as P

HD = 128
ROWS = 128
SPAN = 2 * ROWS
PAIR = 2 * HD
MSG = PAIR + 16
PIECE = 8
F32 = jnp.float32
BF16 = jnp.bfloat16
NEVER = -1e30


def dot(a, b, dims=((1,), (0,))):
    return lax.dot_general(a, b, (dims, ((), ())), preferred_element_type=F32)


def three(x):
    first = x.astype(BF16)
    rest = x - first.astype(F32)
    second = rest.astype(BF16)
    third = (rest - second.astype(F32)).astype(BF16)
    return first.astype(F32), second.astype(F32), third.astype(F32)


def tile_of(rows):
    at = lax.broadcasted_iota(jnp.int32, (16, HD), 0)
    tile = jnp.zeros((16, HD), F32)
    for u, row in enumerate(rows):
        for part, value in enumerate(three(row)):
            tile = jnp.where(at == 8 * u + part, value, tile)
    return tile.astype(BF16)


def row_of(tile, u):
    wide = tile.astype(F32)
    return wide[8 * u : 8 * u + 1] + wide[8 * u + 1 : 8 * u + 2] + wide[8 * u + 2 : 8 * u + 3]


def kernel(
    ns, nz,
    q_ref, k_ref, v_ref, ld_ref, cached_ref, gain_ref,
    att_ref, fin_ref,
    qkv, ld_all, lower, run_all, within,
    l_send, l_recv, x_send, x_recv, e_send, e_recv, s_send, s_recv, out,
    own_sem, in_send, in_recv, ld_sem, l_ss, l_rs, x_ss, x_rs, e_ss, e_rs, s_ss, s_rs, o_own, o_ss, o_rs,
):
    seq = lax.axis_index("seq")
    head = lax.axis_index("head")
    z = lax.div(head, 2)
    core = lax.rem(head, 2)
    other = 1 - core
    partner = 2 * z + other
    mine_rows = pl.ds(pl.multiple_of(core * ROWS, ROWS), ROWS)
    other_rows = pl.ds(pl.multiple_of(other * ROWS, ROWS), ROWS)
    sources = (k_ref, v_ref, q_ref)

    def columns(block, which):
        return pl.ds(pl.multiple_of((2 * block + which) * PAIR, PAIR), PAIR)

    def order(t):
        return lax.rem(z + 1 + t, nz)

    def own_copy(a, b):
        return pltpu.make_async_copy(
            sources[a].at[:, columns(b, core)], qkv.at[a, b, mine_rows], own_sem.at[a, b]
        )

    def swap_copy(a, b):
        return pltpu.make_async_remote_copy(
            sources[a].at[:, columns(b, other)], qkv.at[a, b, mine_rows],
            in_send.at[a, b], in_recv.at[a, b],
            device_id=(seq, partner), device_id_type=pl.DeviceIdType.MESH,
        )

    def swap_arrival(a, b):
        return pltpu.make_async_remote_copy(
            sources[a].at[:, columns(b, other)], qkv.at[a, b, other_rows],
            in_send.at[a, b], in_recv.at[a, b],
            device_id=(seq, partner), device_id_type=pl.DeviceIdType.MESH,
        )

    ld_copy = pltpu.make_async_remote_copy(
        ld_all.at[mine_rows], ld_all.at[mine_rows], ld_sem.at[0], ld_sem.at[1],
        device_id=(seq, partner), device_id_type=pl.DeviceIdType.MESH,
    )
    ld_arrival = pltpu.make_async_remote_copy(
        ld_all.at[other_rows], ld_all.at[other_rows], ld_sem.at[0], ld_sem.at[1],
        device_id=(seq, partner), device_id_type=pl.DeviceIdType.MESH,
    )

    def over_z(src, dst, ss, rs, to, slot):
        return pltpu.make_async_remote_copy(
            src.at[to], dst.at[slot], ss.at[to], rs.at[slot],
            device_id=(seq, 2 * to + core), device_id_type=pl.DeviceIdType.MESH,
        )

    def over_seq(src, dst, ss, rs, to, slot):
        return pltpu.make_async_remote_copy(
            src.at[to], dst.at[slot], ss.at[to], rs.at[slot],
            device_id=(to, head), device_id_type=pl.DeviceIdType.MESH,
        )

    barrier = pltpu.get_barrier_semaphore()
    pl.semaphore_signal(barrier, inc=1, device_id=(seq, partner), device_id_type=pl.DeviceIdType.MESH)

    @pl.loop(1, nz)
    def _(t):
        pl.semaphore_signal(
            barrier, inc=1, device_id=(seq, 2 * lax.rem(z + t, nz) + core), device_id_type=pl.DeviceIdType.MESH
        )

    @pl.loop(1, ns)
    def _(t):
        pl.semaphore_signal(
            barrier, inc=1, device_id=(lax.rem(seq + t, ns), head), device_id_type=pl.DeviceIdType.MESH
        )

    for a in range(3):
        @pl.loop(0, nz)
        def _(t):
            own_copy(a, order(t)).start()

    wide = dot(
        ld_ref[...],
        (lax.broadcasted_iota(jnp.int32, (ld_ref.shape[1], HD), 0)
         == lax.broadcasted_iota(jnp.int32, (ld_ref.shape[1], HD), 1)).astype(F32).astype(BF16),
    )
    ld_all[mine_rows, :] = wide.astype(BF16)
    causal = lax.broadcasted_iota(jnp.int32, (SPAN, SPAN), 0) >= lax.broadcasted_iota(jnp.int32, (SPAN, SPAN), 1)
    lower[...] = causal.astype(F32).astype(BF16)

    pl.semaphore_wait(barrier, 1 + (nz - 1) + (ns - 1))

    ld_copy.start()
    for a in range(3):
        @pl.loop(0, nz)
        def _(t):
            swap_copy(a, order(t)).start()

    ld_copy.wait_send()
    ld_arrival.wait_recv()

    @pl.loop(0, nz)
    def _(t):
        b = order(t)
        for a in range(2):
            own_copy(a, b).wait()
            swap_arrival(a, b).wait_recv()
        ends = []
        for u in range(2):
            which = 4 * b + 2 * core + u
            pick = (lax.broadcasted_iota(jnp.int32, (HD, HD), 0) == which).astype(F32).astype(BF16)
            token = dot(ld_all[...], pick).astype(BF16)
            run = dot(lower[...], token)
            run_all[2 * b + u] = run
            end = run[SPAN - 1 : SPAN]
            ends.append(end)
            keys = qkv[0, b, :, u * HD : (u + 1) * HD].astype(F32)
            scaled = keys * jnp.exp(end - run)
            high = scaled.astype(BF16)
            low = (scaled - high.astype(F32)).astype(BF16)
            both = dot(
                jnp.concatenate([high, low], axis=1), qkv[1, b, :, u * HD : (u + 1) * HD], ((0,), (0,))
            )
            l_send[b, u * HD : (u + 1) * HD, :] = (both[:HD] + both[HD:]).astype(BF16)
        l_send[b, PAIR:MSG, :] = tile_of(ends)

        @pl.when(t < nz - 1)
        def _():
            over_z(l_send, l_recv, l_ss, l_rs, b, z).start()

    l_recv[z] = l_send[z]

    def inside(b):
        own_copy(2, b).wait()
        swap_arrival(2, b).wait_recv()
        for u in range(2):
            which = 4 * b + 2 * core + u
            pick = (lax.broadcasted_iota(jnp.int32, (8, HD), 1) == which).astype(F32).astype(BF16)
            token = dot(pick, ld_all[...], ((1,), (1,))).astype(BF16)
            across = dot(token, lower[...], ((1,), (1,)))[:1]
            run = run_all[2 * b + u]
            keys = qkv[0, b, :, u * HD : (u + 1) * HD]
            queries = qkv[2, b, :, u * HD : (u + 1) * HD]
            values = qkv[1, b, :, u * HD : (u + 1) * HD]
            scores = dot(queries, keys, ((1,), (1,)))
            gap = jnp.concatenate([run, run], axis=1) - across
            here = (
                lax.broadcasted_iota(jnp.int32, (SPAN, SPAN), 0)
                >= lax.broadcasted_iota(jnp.int32, (SPAN, SPAN), 1)
            )
            weights = (scores * jnp.exp(jnp.where(here, gap, NEVER))).astype(BF16)
            within[2 * b + u] = dot(weights, values)

    @pl.loop(0, nz)
    def _(t):
        inside(t)

    first4 = lax.broadcasted_iota(jnp.int32, (8, HD), 0) < 4

    def add(b, sums):
        @pl.when(b != z)
        def _():
            over_z(l_send, l_recv, l_ss, l_rs, b, b).wait_recv()

        tile = l_recv[b, PAIR:MSG, :]
        after = []
        for u in range(2):
            decay, state = sums[2 * u], sums[2 * u + 1]
            step = row_of(tile, u)
            after += [decay + step, jnp.exp(step) * state + l_recv[b, u * HD : (u + 1) * HD, :].astype(F32)]
        return tuple(after)

    none = (jnp.zeros((1, HD), F32), jnp.zeros((HD, HD), F32)) * 2
    decay0, state0, decay1, state1 = lax.fori_loop(0, nz, add, none)
    decays = jnp.where(first4, decay0, decay1)
    for g in range(ns // 2):
        top, bottom = state0[8 * g : 8 * g + 8], state1[8 * g : 8 * g + 8]
        x_send[2 * g, 0:8, :] = jnp.where(first4, top, pltpu.roll(bottom, 4, 0))
        x_send[2 * g + 1, 0:8, :] = jnp.where(first4, pltpu.roll(top, 4, 0), bottom)
        x_send[2 * g, 8:16, :] = decays
        x_send[2 * g + 1, 8:16, :] = decays

    @pl.loop(1, ns)
    def _(t):
        over_seq(x_send, x_recv, x_ss, x_rs, lax.rem(seq + t, ns), seq).start()

    x_recv[seq] = x_send[seq]

    at = pl.ds(pl.multiple_of(lax.div(seq, 2) * 8, 8), 8)
    top, bottom = cached_ref[0, at, :], cached_ref[1, at, :]
    even = jnp.where(first4, top, pltpu.roll(bottom, 4, 0))
    odd = jnp.where(first4, pltpu.roll(top, 4, 0), bottom)
    start = jnp.where(lax.rem(seq, 2) == 0, even, odd)

    def through(i, piece):
        @pl.when(i != seq)
        def _():
            over_seq(x_send, x_recv, x_ss, x_rs, i, i).wait_recv()

        e_send[i] = piece

        @pl.when(i != seq)
        def _():
            over_seq(e_send, e_recv, e_ss, e_rs, i, seq).start()

        return jnp.exp(x_recv[i, 8:16, :]) * piece + x_recv[i, 0:8, :]

    last = lax.fori_loop(0, ns, through, start)
    fin_ref[0] = last[0:4]
    fin_ref[1] = last[4:8]
    e_recv[seq] = e_send[seq]

    @pl.loop(1, ns)
    def _(t):
        over_seq(e_send, e_recv, e_ss, e_rs, lax.rem(seq + t, ns), lax.rem(seq + t, ns)).wait_recv()

    tops, bottoms = [], []
    for g in range(ns // 2):
        even, odd = e_recv[2 * g], e_recv[2 * g + 1]
        tops.append(jnp.where(first4, even, pltpu.roll(odd, 4, 0)))
        bottoms.append(jnp.where(first4, pltpu.roll(even, 4, 0), odd))
    entry = (jnp.concatenate(tops, axis=0), jnp.concatenate(bottoms, axis=0))
    gains = tile_of([gain_ref[0:1, :], gain_ref[1:2, :]])

    def give(b, states):
        tile = l_recv[b, PAIR:MSG, :]
        after = []
        for u in range(2):
            s_send[b, u * HD : (u + 1) * HD, :] = states[u].astype(BF16)
            after.append(
                jnp.exp(row_of(tile, u)) * states[u] + l_recv[b, u * HD : (u + 1) * HD, :].astype(F32)
            )
        s_send[b, PAIR:MSG, :] = gains

        @pl.when(b != z)
        def _():
            over_z(s_send, s_recv, s_ss, s_rs, b, z).start()

        return tuple(after)

    lax.fori_loop(0, nz, give, entry)
    s_recv[z] = s_send[z]

    def out_own(b):
        return pltpu.make_async_copy(out.at[b, mine_rows], att_ref.at[:, columns(b, core)], o_own.at[b])

    def out_swap(b):
        return pltpu.make_async_remote_copy(
            out.at[b, other_rows], att_ref.at[:, columns(b, core)], o_ss.at[b], o_rs.at[b],
            device_id=(seq, partner), device_id_type=pl.DeviceIdType.MESH,
        )

    def out_arrival(b):
        return pltpu.make_async_remote_copy(
            out.at[b, other_rows], att_ref.at[:, columns(b, other)], o_ss.at[b], o_rs.at[b],
            device_id=(seq, partner), device_id_type=pl.DeviceIdType.MESH,
        )

    @pl.loop(0, nz)
    def _(t):
        b = lax.rem(z + t, nz)

        @pl.when(t > 0)
        def _():
            over_z(s_send, s_recv, s_ss, s_rs, b, b).wait_recv()

        tile = s_recv[b, PAIR:MSG, :]
        for u in range(2):
            queries = qkv[2, b, :, u * HD : (u + 1) * HD]
            carried = dot(queries, s_recv[b, u * HD : (u + 1) * HD, :])
            mixed = within[2 * b + u] + carried * jnp.exp(run_all[2 * b + u])
            mean = jnp.mean(mixed * mixed, axis=1, keepdims=True)
            normed = mixed * lax.rsqrt(mean + 1e-6) * row_of(tile, u)
            out[b, :, u * HD : (u + 1) * HD] = normed.astype(BF16)
        out_own(b).start()
        out_swap(b).start()

    for a in range(3):
        @pl.loop(0, nz)
        def _(t):
            swap_copy(a, t).wait_send()

    @pl.loop(1, nz)
    def _(t):
        b = lax.rem(z + t, nz)
        over_z(l_send, l_recv, l_ss, l_rs, b, z).wait_send()
        over_z(s_send, s_recv, s_ss, s_rs, b, z).wait_send()

    @pl.loop(1, ns)
    def _(t):
        i = lax.rem(seq + t, ns)
        over_seq(x_send, x_recv, x_ss, x_rs, i, seq).wait_send()
        over_seq(e_send, e_recv, e_ss, e_rs, i, seq).wait_send()

    @pl.loop(0, nz)
    def _(b):
        out_own(b).wait()
        out_swap(b).wait_send()
        out_arrival(b).wait_recv()


def local(ns, nz, queries, keys, values, log_decay, cached_state, norm_gain):
    anywhere = pl.BlockSpec(memory_space=pl.ANY)
    vmem = pl.BlockSpec(memory_space=pltpu.VMEM)
    dma = pltpu.SemaphoreType.DMA
    return pl.pallas_call(
        functools.partial(kernel, ns, nz),
        out_shape=(
            jax.ShapeDtypeStruct(queries.shape, BF16),
            jax.ShapeDtypeStruct((2, HD // ns, HD), F32),
        ),
        in_specs=[anywhere, anywhere, anywhere, vmem, vmem, vmem],
        out_specs=(anywhere, vmem),
        scratch_shapes=[
            pltpu.VMEM((3, nz, SPAN, PAIR), BF16),
            pltpu.VMEM((SPAN, HD), BF16),
            pltpu.VMEM((SPAN, SPAN), BF16),
            pltpu.VMEM((2 * nz, SPAN, HD), F32),
            pltpu.VMEM((2 * nz, SPAN, HD), F32),
            pltpu.VMEM((nz, MSG, HD), BF16),
            pltpu.VMEM((nz, MSG, HD), BF16),
            pltpu.VMEM((ns, 16, HD), F32),
            pltpu.VMEM((ns, 16, HD), F32),
            pltpu.VMEM((ns, PIECE, HD), F32),
            pltpu.VMEM((ns, PIECE, HD), F32),
            pltpu.VMEM((nz, MSG, HD), BF16),
            pltpu.VMEM((nz, MSG, HD), BF16),
            pltpu.VMEM((nz, SPAN, PAIR), BF16),
            dma((3, nz)), dma((3, nz)), dma((3, nz)), dma((2,)),
            dma((nz,)), dma((nz,)), dma((ns,)), dma((ns,)), dma((ns,)), dma((ns,)),
            dma((nz,)), dma((nz,)), dma((nz,)), dma((nz,)), dma((nz,)),
        ],
        compiler_params=pltpu.CompilerParams(
            collective_id=0, has_side_effects=True, vmem_limit_bytes=60 * 1024 * 1024
        ),
        cost_estimate=pl.CostEstimate(flops=10**9, bytes_accessed=8 * 2**20, transcendentals=2 * 10**6),
    )(queries, keys, values, log_decay, cached_state, norm_gain)


def solution(mesh):
    rows = P(("seq", "head"), None)
    return jax.shard_map(
        functools.partial(local, mesh.shape["seq"], mesh.shape["head"] // 2),
        mesh=mesh,
        in_specs=(rows, rows, rows, rows, P("head", None, None), P("head", None)),
        out_specs=(rows, P("head", "seq", None)),
        check_vma=False,
    )
```

time: 450 us -> 74.8 us (0.17); the launches traced: 445 us -> 74.6 us
  waiting for transfers between devices: 199 us -> 0 us
  other arithmetic: 85.9 us -> 0 us
  Pallas kernels: 0 us -> 69.7 us
  blocking collectives: 62.7 us -> 0 us
  starting transfers between devices: 43.7 us -> 0 us
  local copies, waits for them, and re-layouts: 26.5 us -> 4.3 us
  between operations: 15 us -> 0.65 us
  matrix products: 11.2 us -> 0 us
    psum x1 -> x0, waiting for transfers between devices: 145 us -> none  [broadcast(): return lax.psum(kept, axis)]
    select_n x65 -> x0, other arithmetic: 73.9 us -> none  [the longest x64 72.3 us: step(): return jax.tree.map(lambda a, b: jnp.where(reached, a, b), new, before)]
    pallas_call x0 -> x1, Pallas kernels: none -> 69.7 us  [local(): pl.pallas_call(functools.partial(kernel, ns, nz), out_shape=(jax.ShapeDty...]
    unnamed x1 -> x0, blocking collectives: 62.7 us -> none
    all_to_all x5 -> x0, waiting for transfers between devices: 53.3 us -> none  [the longest x1 26.9 us: local(): lax.all_to_all(keys, 'head', split_axis=1, concat_axis=0, tiled=True)]
    all_to_all x5 -> x0, starting transfers between devices: 43.6 us -> none  [the longest x1 20.6 us: local(): lax.all_to_all(rounded, 'head', split_axis=0, concat_axis=1, tiled=True)]
    dot_general x3 -> x0, matrix products: 11.2 us -> none  [the longest x1 6.36 us: local(): jnp.einsum('bhts,bshd->bthd', weights, value_blocks, preferred_element_ty...]
    all_to_all x5 -> x0, local copies, waits for them, and re-layouts: 7.91 us -> none  [the longest x1 2.39 us: local(): lax.all_to_all(keys, 'head', split_axis=1, concat_axis=0, tiled=True)]
  transfers between devices with their start and end apart: 7 -> 0, of which waited for: 4 -> 0; matrix products, arithmetic and copies ran while one was open for 6% -> 0% of each run, Pallas kernels for 0% -> 0%
where the time goes in v1:
time: 74.8 us; the launch traced here: 74.6 us
  Pallas kernels  69.7 us (93%)
  local copies, waits for them, and re-layouts  4.3 us (6%)
    pallas_call x1, Pallas kernels, local(): pl.pallas_call(functools.partial(kernel, ns, nz), out_shape=(jax.ShapeDty...  69.7 us
    unnamed x5, local copies, waits for them, and re-layouts  4.3 us

profile of v1, /device:TPU:1, one launch (start us, length us, event | category | flops | bytes accessed | tf_op | source)
XLA Modules:
  0.0 74.6 jit_solution(3015728919647220075)
XLA Ops:
  0.6 1.4 %copy.8.ld_ref = bf16[128,32]{1,0:T(8,128)(2,1)} copy(bf16[128,32]{0,1:T(8,128)(2,1)} %param.9) | data formatting | bytes 16384 | tf_op args[3]
  2.0 69.7 %shard_map.77 = (bf16[128,4096]{1,0:T(8,128)(2,1)}, f32[2,4,128]{2,1,0:T(4,128)}) custom-call(bf16[128,4096]{1,0:T(8,128)(2,1)} %q_ref.1, bf16[128,4096]{1,0:T(8,128)(2,1)} %k_ref.1, bf16[128,4096]{1,0:T(8,128)(2,1)} %v_ref.1, bf16[128,32]{1,0:T(8,128)(2,1)} %copy.8.ld_ref, f32[2,128,128]{2,1,0:T(8,128)} %cached_ref.1, f32[2,128]{1,0:T(2,128)} %gain_ref.1), custom_call_target="tpu_custom_call" | custom-call | flops 1000000000 | bytes 8388608 | tf_op jit(solution)/shard_map/pallas_call | solution.py:355
  71.7 0.0 copy-start
  71.7 2.3 %copy.11 = bf16[128,4096]{1,0:T(8,128)(2,1)} copy(bf16[128,4096]{1,0:T(8,128)(2,1)} %get-tuple-element.4) | data formatting | bytes 2097152
  74.0 0.0 copy-done
  74.0 0.6 copy.12
Async XLA Ops:
  71.7 2.3 %copy-start = (f32[2,4,128]{2,1,0:T(4,128)S(1)}, f32[2,4,128]{2,1,0:T(4,128)}, u32[]{:S(2)}) copy-start(f32[2,4,128]{2,1,0:T(4,128)} %get-tuple-element.5) | copy-start | bytes 12292

commit v2 on v0

v2 whole, which is shorter than its diff:
```python
import functools

import jax
import jax.numpy as jnp
from jax import lax
from jax.experimental import pallas as pl
from jax.experimental.pallas import tpu as pltpu
from jax.sharding import PartitionSpec as P

HD = 128
ROWS = 128
SPAN = 2 * ROWS
PAIR = 2 * HD
HALF = HD // 2
PIECE = 8
F32 = jnp.float32
BF16 = jnp.bfloat16
NEVER = -1e30
MESH = pl.DeviceIdType.MESH


def dot(a, b, dims=((1,), (0,))):
    return lax.dot_general(a, b, (dims, ((), ())), preferred_element_type=F32)


def kernel(
    ns, nz,
    q_ref, k_ref, v_ref, ld_ref, cached_ref, gain_ref,
    att_ref, fin_ref,
    tokens, ld_all, decay_rows, run_rows, fade_rows, end_rows, lower, run_all, within,
    l_send, l_recv, x_send, x_recv, e_send, e_recv, s_send, s_recv, out, fin_all, cached, gain, z_send, z_recv, d_send, d_recv,
    own_sem, in_send, in_recv, ld_sem, l_ss, l_rs, x_ss, x_rs, e_ss, e_rs, s_ss, s_rs, o_own, o_ss, o_rs, f_sem, small_sem,
    z_ss, z_rs, d_ss, d_rs,
):
    seq = lax.axis_index("seq")
    head = lax.axis_index("head")
    z = lax.div(head, 2)
    core = lax.rem(head, 2)
    other = 1 - core
    partner = 2 * z + other
    group = lax.div(seq, 2)
    turn = lax.rem(seq, 2)
    sources = (k_ref, v_ref, q_ref)

    def columns(block, which):
        return pl.ds(pl.multiple_of((2 * block + which) * PAIR, PAIR), PAIR)

    def head_columns(block, u):
        return pl.ds(pl.multiple_of((2 * block + core) * PAIR + u * HD, HD), HD)

    def rows_of(a, block, u):
        at = head_columns(block, u)
        return jnp.concatenate([tokens[a, 0, :, at], tokens[a, 1, :, at]], axis=0)

    def near(t):
        step = lax.div(t + 1, 2)
        return lax.rem(z + jnp.where(lax.rem(t, 2) == 1, step, nz - step), nz)

    def order(t):
        return near(nz - 1 - t)

    def own_copy(a):
        return pltpu.make_async_copy(sources[a], tokens.at[a, core], own_sem.at[a])

    def to_partner(src, dst, ss, rs):
        return pltpu.make_async_remote_copy(
            src, dst, ss, rs, device_id=(seq, partner), device_id_type=MESH
        )

    def swap_copy(a, b):
        at = columns(b, other)
        return to_partner(sources[a].at[:, at], tokens.at[a, core, :, at], in_send.at[a, b], in_recv.at[a, b])

    def swap_arrival(a, b):
        at = columns(b, core)
        return to_partner(sources[a].at[:, at], tokens.at[a, other, :, at], in_send.at[a, b], in_recv.at[a, b])

    ld_copy = to_partner(ld_all.at[core], ld_all.at[core], ld_sem.at[0], ld_sem.at[1])
    ld_arrival = to_partner(ld_all.at[other], ld_all.at[other], ld_sem.at[0], ld_sem.at[1])

    part_rows = (pl.ds(0, HALF), pl.ds(HALF, HALF))
    near_ns = ns // 4

    def over_z(src, dst, ss, rs, u, part, to, slot):
        return pltpu.make_async_remote_copy(
            src.at[u, to, part_rows[part]], dst.at[u, slot, part_rows[part]],
            ss.at[u, part, to], rs.at[u, part, slot],
            device_id=(seq, 2 * to + core), device_id_type=MESH,
        )

    def facts_copy(to, slot):
        return pltpu.make_async_remote_copy(
            z_send.at[to], z_recv.at[slot], z_ss.at[to], z_rs.at[slot],
            device_id=(seq, 2 * to + core), device_id_type=MESH,
        )

    def decay_copy(to, slot):
        return pltpu.make_async_remote_copy(
            d_send.at[lax.rem(to, 2)], d_recv.at[slot], d_ss.at[to], d_rs.at[slot],
            device_id=(to, head), device_id_type=MESH,
        )

    def piece_rows(g):
        return pl.ds(pl.multiple_of(g * PIECE, PIECE), PIECE)

    def sum_copy(u, g, slot):
        return pltpu.make_async_remote_copy(
            x_send.at[u, g], x_recv.at[slot], x_ss.at[u, g], x_rs.at[slot],
            device_id=(2 * g + u, head), device_id_type=MESH,
        )

    def entry_copy(u, g, to):
        return pltpu.make_async_remote_copy(
            e_send.at[to], e_recv.at[u, piece_rows(g)], e_ss.at[to], e_rs.at[u, g],
            device_id=(to, head), device_id_type=MESH,
        )

    barrier = pltpu.get_barrier_semaphore()
    pl.semaphore_signal(barrier, inc=1, device_id=(seq, partner), device_id_type=MESH)

    @pl.loop(1, nz)
    def _(t):
        pl.semaphore_signal(
            barrier, inc=1, device_id=(seq, 2 * lax.rem(z + t, nz) + core), device_id_type=MESH
        )

    @pl.loop(1, ns)
    def _(t):
        pl.semaphore_signal(barrier, inc=1, device_id=(lax.rem(seq + t, ns), head), device_id_type=MESH)

    ld_own = pltpu.make_async_copy(ld_ref, ld_all.at[core], small_sem.at[0])
    cached_own = pltpu.make_async_copy(cached_ref.at[turn, piece_rows(group)], cached, small_sem.at[1])
    gain_own = pltpu.make_async_copy(gain_ref, gain, small_sem.at[2])
    ld_own.start()
    for a in range(3):
        own_copy(a).start()
    cached_own.start()
    gain_own.start()
    causal = lax.broadcasted_iota(jnp.int32, (SPAN, SPAN), 0) >= lax.broadcasted_iota(jnp.int32, (SPAN, SPAN), 1)
    lower[...] = causal.astype(F32).astype(BF16)

    ld_own.wait()
    pl.semaphore_wait(barrier, 1 + (nz - 1) + (ns - 1))

    ld_copy.start()

    @pl.loop(0, nz)
    def _(t):
        for a in range(2):
            swap_copy(a, order(t)).start()

    def swaps_done():
        ld_copy.wait_send()

        @pl.loop(0, nz)
        def _(t):
            for a in range(3):
                swap_copy(a, t).wait_send()

    ld_arrival.wait_recv()
    for half in range(2):
        decay_rows[:, half * ROWS : (half + 1) * ROWS] = ld_all[half].astype(F32)
    run = dot(decay_rows[...].astype(BF16), lower[...], ((1,), (1,)))
    run_rows[...] = run
    fade_rows[...] = jnp.exp(run[:, SPAN - 1 : SPAN] - run)
    end_rows[...] = jnp.broadcast_to(run[:, SPAN - 1 : SPAN], end_rows.shape)
    gain_own.wait()

    @pl.loop(0, nz)
    def _(t):
        b = order(t)
        first = 4 * b + 2 * core
        at = lax.broadcasted_iota(jnp.int32, (8, HD), 0)
        tile = jnp.where(at == 0, end_rows[pl.ds(first, 1), :], end_rows[pl.ds(first + 1, 1), :])
        z_send[b] = jnp.where(at < 2, tile, jnp.where(at == 2, gain[0:1, :], gain[1:2, :]))

        @pl.when(t < nz - 1)
        def _():
            facts_copy(b, z).start()

    z_recv[z] = z_send[z]
    for a in range(2):
        own_copy(a).wait()

    def send_part(u, part):
        @pl.loop(0, nz - 1)
        def _(t):
            over_z(l_send, l_recv, l_ss, l_rs, u, part, order(t), z).start()

    for u in range(2):
        @pl.loop(0, nz)
        def _(t):
            b = order(t)
            if u == 0:
                for a in range(2):
                    swap_arrival(a, b).wait_recv()
            which = pl.ds(4 * b + 2 * core + u, 1)
            scaled = rows_of(0, b, u).T.astype(F32) * fade_rows[which, :]
            high = scaled.astype(BF16)
            low = (scaled - high.astype(F32)).astype(BF16)
            both = dot(jnp.concatenate([high, low], axis=0), rows_of(1, b, u))
            state = (both[:HD] + both[HD:]).astype(BF16)
            l_send[u, b] = state

            @pl.when(t < nz - 1)
            def _():
                over_z(l_send, l_recv, l_ss, l_rs, u, 0, b, z).start()

        send_part(u, 1)
        l_recv[u, z] = l_send[u, z]
        if u == 0:
            @pl.loop(0, nz)
            def _(t):
                swap_copy(2, t).start()

            @pl.loop(1, nz)
            def _(t):
                facts_copy(lax.rem(z + t, nz), lax.rem(z + t, nz)).wait_recv()

            total = lax.fori_loop(0, nz, lambda b, sums: sums + z_recv[b], jnp.zeros((8, HD), F32))
            for v in range(2):
                d_send[v] = jnp.broadcast_to(total[v : v + 1], (PIECE, HD))

            @pl.loop(1, ns)
            def _(t):
                decay_copy(lax.rem(seq + t, ns), seq).start()

            d_recv[seq] = d_send[turn]

    def l_done():
        @pl.loop(1, nz)
        def _(t):
            for u in range(2):
                for part in range(2):
                    over_z(l_send, l_recv, l_ss, l_rs, u, part, lax.rem(z + t, nz), z).wait_send()

    own_copy(2).wait()

    def inside(b):
        swap_arrival(2, b).wait_recv()
        for u in range(2):
            which = pl.ds(4 * b + 2 * core + u, 1)
            token = jnp.broadcast_to(decay_rows[which, :], (HD, SPAN)).astype(BF16)
            run = dot(lower[...], token, ((1,), (1,)))
            run_all[2 * b + u] = run
            scores = dot(rows_of(2, b, u), rows_of(0, b, u), ((1,), (1,)))
            gap = jnp.concatenate([run, run], axis=1) - run_rows[which, :]
            here = (
                lax.broadcasted_iota(jnp.int32, (SPAN, SPAN), 0)
                >= lax.broadcasted_iota(jnp.int32, (SPAN, SPAN), 1)
            )
            weights = (scores * jnp.exp(jnp.where(here, gap, NEVER))).astype(BF16)
            within[2 * b + u] = dot(weights, rows_of(1, b, u))

    pl.loop(0, nz // 2)(inside)

    def column_sum(u, part):
        def add(b, sums):
            @pl.when(b != z)
            def _():
                over_z(l_send, l_recv, l_ss, l_rs, u, part, b, b).wait_recv()

            return jnp.exp(z_recv[b, u : u + 1, :]) * sums + l_recv[u, b, part_rows[part], :].astype(F32)

        state = lax.fori_loop(0, nz, add, jnp.zeros((HALF, HD), F32))
        for g in range(near_ns):
            x_send[u, near_ns * part + g] = state[PIECE * g : PIECE * (g + 1)]

        @pl.loop(0, near_ns)
        def _(t):
            g = near_ns * part + lax.rem(group + 1 + t, near_ns)

            @pl.when(2 * g + u != seq)
            def _():
                sum_copy(u, g, seq).start()

        @pl.when((turn == u) & (lax.div(group, near_ns) == part))
        def _():
            x_recv[seq] = x_send[u, group]

    def columns_scan(u, part):
        @pl.when((turn == u) & (lax.div(group, near_ns) == part))
        def _():
            @pl.loop(1, ns)
            def _(t):
                sum_copy(u, group, lax.rem(seq + t, ns)).wait_recv()

            piece = cached[...]
            for i in range(ns):
                e_send[i] = piece
                piece = jnp.exp(d_recv[i]) * piece + x_recv[i]
            fin_all[u] = piece

            @pl.loop(0, ns)
            def _(t):
                i = lax.rem(seq + t + 3 * ns // 8, ns)

                @pl.when(i != seq)
                def _():
                    entry_copy(u, group, i).start()

            e_recv[u, piece_rows(group), :] = e_send[seq]

    def give(u, part):
        @pl.loop(near_ns * part, near_ns * (part + 1))
        def _(g):
            @pl.when(2 * g + u != seq)
            def _():
                entry_copy(u, g, seq).wait_recv()

        def step(b, state):
            s_send[u, b, part_rows[part], :] = state.astype(BF16)
            return jnp.exp(z_recv[b, u : u + 1, :]) * state + l_recv[u, b, part_rows[part], :].astype(F32)

        lax.fori_loop(0, nz, step, e_recv[u, HALF * part : HALF * (part + 1), :])

        @pl.loop(0, nz - 1)
        def _(t):
            over_z(s_send, s_recv, s_ss, s_rs, u, part, order(t), z).start()

        if part == 1:
            s_recv[u, z] = s_send[u, z]

    column_sum(0, 0)
    column_sum(0, 1)
    pl.loop(nz // 2, nz)(inside)
    cached_own.wait()

    @pl.loop(1, ns)
    def _(t):
        decay_copy(lax.rem(seq + t, ns), lax.rem(seq + t, ns)).wait_recv()

    columns_scan(0, 0)
    column_sum(1, 0)
    columns_scan(0, 1)
    column_sum(1, 1)
    give(0, 0)
    columns_scan(1, 0)
    give(0, 1)
    columns_scan(1, 1)
    give(1, 0)
    swaps_done()
    l_done()
    give(1, 1)

    def scan_done():
        @pl.loop(0, ns // 2)
        def _(g):
            for u in range(2):
                @pl.when(2 * g + u != seq)
                def _():
                    sum_copy(u, g, seq).wait_send()

        @pl.loop(1, ns)
        def _(t):
            i = lax.rem(seq + t, ns)
            decay_copy(i, seq).wait_send()
            entry_copy(0, group, i).wait_send()

        @pl.loop(1, nz)
        def _(t):
            facts_copy(lax.rem(z + t, nz), z).wait_send()

    def s_done():
        @pl.loop(1, nz)
        def _(t):
            for u in range(2):
                for part in range(2):
                    over_z(s_send, s_recv, s_ss, s_rs, u, part, lax.rem(z + t, nz), z).wait_send()

    def fin_copy(slot):
        return pltpu.make_async_remote_copy(
            fin_all.at[slot], fin_all.at[slot], f_sem.at[0], f_sem.at[1],
            device_id=(2 * group + 1 - turn, head), device_id_type=MESH,
        )

    fin_copy(turn).start()

    mine_rows = pl.ds(pl.multiple_of(core * ROWS, ROWS), ROWS)
    other_rows = pl.ds(pl.multiple_of(other * ROWS, ROWS), ROWS)

    def out_own(b):
        return pltpu.make_async_copy(out.at[b, mine_rows], att_ref.at[:, columns(b, core)], o_own.at[b])

    def out_swap(b):
        return to_partner(out.at[b, other_rows], att_ref.at[:, columns(b, core)], o_ss.at[b], o_rs.at[b])

    def out_arrival(b):
        return to_partner(out.at[b, other_rows], att_ref.at[:, columns(b, other)], o_ss.at[b], o_rs.at[b])

    def output(u):
        @pl.loop(0, nz)
        def _(t):
            b = near(t)

            @pl.when(t > 0)
            def _():
                for part in range(2):
                    over_z(s_send, s_recv, s_ss, s_rs, u, part, b, b).wait_recv()

            carried = dot(rows_of(2, b, u), s_recv[u, b])
            mixed = within[2 * b + u] + carried * jnp.exp(run_all[2 * b + u])
            mean = jnp.mean(mixed * mixed, axis=1, keepdims=True)
            normed = mixed * lax.rsqrt(mean + 1e-6) * z_recv[b, 2 + u : 3 + u, :]
            out[b, :, u * HD : (u + 1) * HD] = normed.astype(BF16)
            if u == 1:
                out_own(b).start()
                out_swap(b).start()

    output(0)
    scan_done()
    output(1)
    fin_copy(1 - turn).wait_recv()
    for u in range(2):
        fin_ref[u] = jnp.where(turn == 0, fin_all[u, 0:4, :], fin_all[u, 4:8, :])

    fin_copy(turn).wait_send()
    s_done()

    @pl.loop(0, nz)
    def _(b):
        out_own(b).wait()
        out_swap(b).wait_send()
        out_arrival(b).wait_recv()


def local(ns, nz, queries, keys, values, log_decay, cached_state, norm_gain):
    anywhere = pl.BlockSpec(memory_space=pl.ANY)
    vmem = pl.BlockSpec(memory_space=pltpu.VMEM)
    dma = pltpu.SemaphoreType.DMA
    heads = log_decay.shape[1]
    return pl.pallas_call(
        functools.partial(kernel, ns, nz),
        out_shape=(
            jax.ShapeDtypeStruct(queries.shape, BF16),
            jax.ShapeDtypeStruct((2, HD // ns, HD), F32),
        ),
        in_specs=[anywhere] * 6,
        out_specs=(anywhere, vmem),
        scratch_shapes=[
            pltpu.VMEM((3, 2) + queries.shape, BF16),
            pltpu.VMEM((2, heads, ROWS), BF16),
            pltpu.VMEM((heads, SPAN), F32),
            pltpu.VMEM((heads, SPAN), F32),
            pltpu.VMEM((heads, SPAN), F32),
            pltpu.VMEM((heads, HD), F32),
            pltpu.VMEM((SPAN, SPAN), BF16),
            pltpu.VMEM((2 * nz, SPAN, HD), F32),
            pltpu.VMEM((2 * nz, SPAN, HD), F32),
            pltpu.VMEM((2, nz, HD, HD), BF16),
            pltpu.VMEM((2, nz, HD, HD), BF16),
            pltpu.VMEM((2, ns // 2, PIECE, HD), F32),
            pltpu.VMEM((ns, PIECE, HD), F32),
            pltpu.VMEM((ns, PIECE, HD), F32),
            pltpu.VMEM((2, HD, HD), F32),
            pltpu.VMEM((2, nz, HD, HD), BF16),
            pltpu.VMEM((2, nz, HD, HD), BF16),
            pltpu.VMEM((nz, SPAN, PAIR), BF16),
            pltpu.VMEM((2, PIECE, HD), F32),
            pltpu.VMEM((PIECE, HD), F32),
            pltpu.VMEM((2, HD), F32),
            pltpu.VMEM((nz, 8, HD), F32),
            pltpu.VMEM((nz, 8, HD), F32),
            pltpu.VMEM((2, PIECE, HD), F32),
            pltpu.VMEM((ns, PIECE, HD), F32),
            dma((3,)), dma((3, nz)), dma((3, nz)), dma((2,)),
            dma((2, 2, nz)), dma((2, 2, nz)), dma((2, ns // 2)), dma((ns,)), dma((ns,)), dma((2, ns // 2)),
            dma((2, 2, nz)), dma((2, 2, nz)), dma((nz,)), dma((nz,)), dma((nz,)), dma((2,)), dma((3,)),
            dma((nz,)), dma((nz,)), dma((ns,)), dma((ns,)),
        ],
        compiler_params=pltpu.CompilerParams(
            collective_id=0, has_side_effects=True, vmem_limit_bytes=60 * 1024 * 1024
        ),
        cost_estimate=pl.CostEstimate(flops=10**9, bytes_accessed=8 * 2**20, transcendentals=2 * 10**6),
    )(queries, keys, values, log_decay.T, cached_state, norm_gain)


def solution(mesh):
    rows = P(("seq", "head"), None)
    return jax.shard_map(
        functools.partial(local, mesh.shape["seq"], mesh.shape["head"] // 2),
        mesh=mesh,
        in_specs=(rows, rows, rows, rows, P("head", None, None), P("head", None)),
        out_specs=(rows, P("head", "seq", None)),
        check_vma=False,
    )
```

time: 450 us -> 62.7 us (0.14); the launches traced: 445 us -> 62.5 us
  waiting for transfers between devices: 199 us -> 0 us
  other arithmetic: 85.9 us -> 0 us
  blocking collectives: 62.7 us -> 0 us
  Pallas kernels: 0 us -> 59 us
  starting transfers between devices: 43.7 us -> 0 us
  local copies, waits for them, and re-layouts: 26.5 us -> 2.88 us
  between operations: 15 us -> 0.65 us
  matrix products: 11.2 us -> 0 us
    psum x1 -> x0, waiting for transfers between devices: 145 us -> none  [broadcast(): return lax.psum(kept, axis)]
    select_n x65 -> x0, other arithmetic: 73.9 us -> none  [the longest x64 72.3 us: step(): return jax.tree.map(lambda a, b: jnp.where(reached, a, b), new, before)]
    unnamed x1 -> x0, blocking collectives: 62.7 us -> none
    pallas_call x0 -> x1, Pallas kernels: none -> 59 us  [local(): pl.pallas_call(functools.partial(kernel, ns, nz), out_shape=(jax.ShapeDty...]
    all_to_all x5 -> x0, waiting for transfers between devices: 53.3 us -> none  [the longest x1 26.9 us: local(): lax.all_to_all(keys, 'head', split_axis=1, concat_axis=0, tiled=True)]
    all_to_all x5 -> x0, starting transfers between devices: 43.6 us -> none  [the longest x1 20.6 us: local(): lax.all_to_all(rounded, 'head', split_axis=0, concat_axis=1, tiled=True)]
    dot_general x3 -> x0, matrix products: 11.2 us -> none  [the longest x1 6.36 us: local(): jnp.einsum('bhts,bshd->bthd', weights, value_blocks, preferred_element_ty...]
    all_to_all x5 -> x0, local copies, waits for them, and re-layouts: 7.91 us -> none  [the longest x1 2.39 us: local(): lax.all_to_all(keys, 'head', split_axis=1, concat_axis=0, tiled=True)]
  transfers between devices with their start and end apart: 7 -> 0, of which waited for: 4 -> 0; matrix products, arithmetic and copies ran while one was open for 6% -> 0% of each run, Pallas kernels for 0% -> 0%
where the time goes in v2:
time: 62.7 us; the launch traced here: 62.5 us
  Pallas kernels  59 us (94%)
  local copies, waits for them, and re-layouts  2.88 us (5%)
  between operations  0.65 us (1%)
    pallas_call x1, Pallas kernels, local(): pl.pallas_call(functools.partial(kernel, ns, nz), out_shape=(jax.ShapeDty...  59 us
    unnamed x4, local copies, waits for them, and re-layouts  2.88 us

profile of v2, /device:TPU:1, one launch (start us, length us, event | category | flops | bytes accessed | tf_op | source)
XLA Modules:
  0.0 62.5 jit_solution(15161757605200595706)
XLA Ops:
  0.6 59.0 %shard_map.77 = (bf16[128,4096]{1,0:T(8,128)(2,1)}, f32[2,4,128]{2,1,0:T(4,128)}) custom-call(bf16[128,4096]{1,0:T(8,128)(2,1)} %q_ref.1, bf16[128,4096]{1,0:T(8,128)(2,1)} %k_ref.1, bf16[128,4096]{1,0:T(8,128)(2,1)} %v_ref.1, bf16[32,128]{1,0:T(8,128)(2,1)} %bitcast.1, f32[2,128,128]{2,1,0:T(8,128)} %cached_ref.1, f32[2,128]{1,0:T(2,128)} %gain_ref.1), custom_call_target="tpu_custom_call" | custom-call | flops 1000000000 | bytes 8388608 | tf_op jit(solution)/shard_map/pallas_call | solution.py:432
  59.6 0.0 copy-start
  59.6 2.3 %copy.10 = bf16[128,4096]{1,0:T(8,128)(2,1)} copy(bf16[128,4096]{1,0:T(8,128)(2,1)} %get-tuple-element.4) | data formatting | bytes 2097152
  61.9 0.0 copy-done
  61.9 0.6 copy.11
Async XLA Ops:
  59.6 2.3 %copy-start = (f32[2,4,128]{2,1,0:T(4,128)S(1)}, f32[2,4,128]{2,1,0:T(4,128)}, u32[]{:S(2)}) copy-start(f32[2,4,128]{2,1,0:T(4,128)} %get-tuple-element.5) | copy-start | bytes 12292

commit v3 on v2

--- a/solution.py
+++ b/solution.py
@@ -29,8 +29,7 @@
     att_ref, fin_ref,
     tokens, ld_all, decay_rows, run_rows, fade_rows, end_rows, lower, run_all, within,
     l_send, l_recv, x_send, x_recv, e_send, e_recv, s_send, s_recv, out, fin_all, cached, gain, z_send, z_recv, d_send, d_recv,
-    own_sem, in_send, in_recv, ld_sem, l_ss, l_rs, x_ss, x_rs, e_ss, e_rs, s_ss, s_rs, o_own, o_ss, o_rs, f_sem, small_sem,
-    z_ss, z_rs, d_ss, d_rs,
+    own_sem, in_send, in_recv, ld_sem, l_ss, l_rs, x_sem, e_sem, s_ss, s_rs, o_sem, f_sem, small_sem, z_sem, d_sem,
 ):
     seq = lax.axis_index("seq")
     head = lax.axis_index("head")
@@ -67,13 +66,16 @@
             src, dst, ss, rs, device_id=(seq, partner), device_id_type=MESH
         )
 
+    def arrived(ref, sem):
+        to_partner(ref, ref, sem, sem).wait_recv()
+
+    def sent(ref, sem):
+        to_partner(ref, ref, sem, sem).wait_send()
+
     def swap_copy(a, b):
         at = columns(b, other)
-        return to_partner(sources[a].at[:, at], tokens.at[a, core, :, at], in_send.at[a, b], in_recv.at[a, b])
-
-    def swap_arrival(a, b):
-        at = columns(b, core)
-        return to_partner(sources[a].at[:, at], tokens.at[a, other, :, at], in_send.at[a, b], in_recv.at[a, b])
+        landed = in_recv.at[nz] if a == 2 else in_recv.at[b]
+        return to_partner(sources[a].at[:, at], tokens.at[a, core, :, at], in_send.at[0], landed)
 
     ld_copy = to_partner(ld_all.at[core], ld_all.at[core], ld_sem.at[0], ld_sem.at[1])
     ld_arrival = to_partner(ld_all.at[other], ld_all.at[other], ld_sem.at[0], ld_sem.at[1])
@@ -81,22 +83,22 @@
     part_rows = (pl.ds(0, HALF), pl.ds(HALF, HALF))
     near_ns = ns // 4
 
-    def over_z(src, dst, ss, rs, u, part, to, slot):
+    def over_z(src, dst, ss, rs, u, part, to, slot, by_slot=False):
         return pltpu.make_async_remote_copy(
             src.at[u, to, part_rows[part]], dst.at[u, slot, part_rows[part]],
-            ss.at[u, part, to], rs.at[u, part, slot],
+            ss.at[0], rs.at[3 + slot if by_slot and u == part == 1 else 2 * u + part],
             device_id=(seq, 2 * to + core), device_id_type=MESH,
         )
 
     def facts_copy(to, slot):
         return pltpu.make_async_remote_copy(
-            z_send.at[to], z_recv.at[slot], z_ss.at[to], z_rs.at[slot],
+            z_send.at[to], z_recv.at[slot], z_sem.at[0], z_sem.at[1],
             device_id=(seq, 2 * to + core), device_id_type=MESH,
         )
 
     def decay_copy(to, slot):
         return pltpu.make_async_remote_copy(
-            d_send.at[lax.rem(to, 2)], d_recv.at[slot], d_ss.at[to], d_rs.at[slot],
+            d_send.at[lax.rem(to, 2)], d_recv.at[slot], d_sem.at[0], d_sem.at[1],
             device_id=(to, head), device_id_type=MESH,
         )
 
@@ -105,13 +107,13 @@
 
     def sum_copy(u, g, slot):
         return pltpu.make_async_remote_copy(
-            x_send.at[u, g], x_recv.at[slot], x_ss.at[u, g], x_rs.at[slot],
+            x_send.at[2 * g + u], x_recv.at[slot], x_sem.at[0], x_sem.at[1],
             device_id=(2 * g + u, head), device_id_type=MESH,
         )
 
     def entry_copy(u, g, to):
         return pltpu.make_async_remote_copy(
-            e_send.at[to], e_recv.at[u, piece_rows(g)], e_ss.at[to], e_rs.at[u, g],
+            e_send.at[to], e_recv.at[u, piece_rows(g)], e_sem.at[0], e_sem.at[1 + 2 * u + lax.div(g, near_ns)],
             device_id=(to, head), device_id_type=MESH,
         )
 
@@ -149,13 +151,11 @@
         for a in range(2):
             swap_copy(a, order(t)).start()
 
+    halves = pl.ds(0, nz * PAIR)
+
     def swaps_done():
         ld_copy.wait_send()
-
-        @pl.loop(0, nz)
-        def _(t):
-            for a in range(3):
-                swap_copy(a, t).wait_send()
+        sent(tokens.at[:, 0, :, halves], in_send.at[0])
 
     ld_arrival.wait_recv()
     for half in range(2):
@@ -192,8 +192,7 @@
         def _(t):
             b = order(t)
             if u == 0:
-                for a in range(2):
-                    swap_arrival(a, b).wait_recv()
+                arrived(tokens.at[pl.ds(0, 2), other, :, columns(b, core)], in_recv.at[b])
             which = pl.ds(4 * b + 2 * core + u, 1)
             scaled = rows_of(0, b, u).T.astype(F32) * fade_rows[which, :]
             high = scaled.astype(BF16)
@@ -213,10 +212,7 @@
             def _(t):
                 swap_copy(2, t).start()
 
-            @pl.loop(1, nz)
-            def _(t):
-                facts_copy(lax.rem(z + t, nz), lax.rem(z + t, nz)).wait_recv()
-
+            arrived(z_recv.at[pl.ds(0, nz - 1)], z_sem.at[1])
             total = lax.fori_loop(0, nz, lambda b, sums: sums + z_recv[b], jnp.zeros((8, HD), F32))
             for v in range(2):
                 d_send[v] = jnp.broadcast_to(total[v : v + 1], (PIECE, HD))
@@ -228,16 +224,12 @@
             d_recv[seq] = d_send[turn]
 
     def l_done():
-        @pl.loop(1, nz)
-        def _(t):
-            for u in range(2):
-                for part in range(2):
-                    over_z(l_send, l_recv, l_ss, l_rs, u, part, lax.rem(z + t, nz), z).wait_send()
+        sent(l_send.at[:, pl.ds(0, nz - 1)], l_ss.at[0])
 
     own_copy(2).wait()
+    arrived(tokens.at[2, other, :, halves], in_recv.at[nz])
 
     def inside(b):
-        swap_arrival(2, b).wait_recv()
         for u in range(2):
             which = pl.ds(4 * b + 2 * core + u, 1)
             token = jnp.broadcast_to(decay_rows[which, :], (HD, SPAN)).astype(BF16)
@@ -255,16 +247,14 @@
     pl.loop(0, nz // 2)(inside)
 
     def column_sum(u, part):
+        arrived(l_recv.at[u, pl.ds(0, nz - 1), part_rows[part]], l_rs.at[2 * u + part])
+
         def add(b, sums):
-            @pl.when(b != z)
-            def _():
-                over_z(l_send, l_recv, l_ss, l_rs, u, part, b, b).wait_recv()
-
             return jnp.exp(z_recv[b, u : u + 1, :]) * sums + l_recv[u, b, part_rows[part], :].astype(F32)
 
         state = lax.fori_loop(0, nz, add, jnp.zeros((HALF, HD), F32))
         for g in range(near_ns):
-            x_send[u, near_ns * part + g] = state[PIECE * g : PIECE * (g + 1)]
+            x_send[2 * (near_ns * part + g) + u] = state[PIECE * g : PIECE * (g + 1)]
 
         @pl.loop(0, near_ns)
         def _(t):
@@ -276,15 +266,12 @@
 
         @pl.when((turn == u) & (lax.div(group, near_ns) == part))
         def _():
-            x_recv[seq] = x_send[u, group]
+            x_recv[seq] = x_send[seq]
 
     def columns_scan(u, part):
         @pl.when((turn == u) & (lax.div(group, near_ns) == part))
         def _():
-            @pl.loop(1, ns)
-            def _(t):
-                sum_copy(u, group, lax.rem(seq + t, ns)).wait_recv()
-
+            arrived(x_recv.at[pl.ds(0, ns - 1)], x_sem.at[1])
             piece = cached[...]
             for i in range(ns):
                 e_send[i] = piece
@@ -302,11 +289,16 @@
             e_recv[u, piece_rows(group), :] = e_send[seq]
 
     def give(u, part):
-        @pl.loop(near_ns * part, near_ns * (part + 1))
-        def _(g):
-            @pl.when(2 * g + u != seq)
-            def _():
-                entry_copy(u, g, seq).wait_recv()
+        landed = e_sem.at[1 + 2 * u + part]
+        owner = (turn == u) & (lax.div(group, near_ns) == part)
+
+        @pl.when(owner)
+        def _():
+            arrived(e_recv.at[u, pl.ds(0, HALF - PIECE)], landed)
+
+        @pl.when(jnp.logical_not(owner))
+        def _():
+            arrived(e_recv.at[u, pl.ds(0, HALF)], landed)
 
         def step(b, state):
             s_send[u, b, part_rows[part], :] = state.astype(BF16)
@@ -316,7 +308,7 @@
 
         @pl.loop(0, nz - 1)
         def _(t):
-            over_z(s_send, s_recv, s_ss, s_rs, u, part, order(t), z).start()
+            over_z(s_send, s_recv, s_ss, s_rs, u, part, order(t), z, True).start()
 
         if part == 1:
             s_recv[u, z] = s_send[u, z]
@@ -326,9 +318,7 @@
     pl.loop(nz // 2, nz)(inside)
     cached_own.wait()
 
-    @pl.loop(1, ns)
-    def _(t):
-        decay_copy(lax.rem(seq + t, ns), lax.rem(seq + t, ns)).wait_recv()
+    arrived(d_recv.at[pl.ds(0, ns - 1)], d_sem.at[1])
 
     columns_scan(0, 0)
     column_sum(1, 0)
@@ -344,29 +334,13 @@
     give(1, 1)
 
     def scan_done():
-        @pl.loop(0, ns // 2)
-        def _(g):
-            for u in range(2):
-                @pl.when(2 * g + u != seq)
-                def _():
-                    sum_copy(u, g, seq).wait_send()
-
-        @pl.loop(1, ns)
-        def _(t):
-            i = lax.rem(seq + t, ns)
-            decay_copy(i, seq).wait_send()
-            entry_copy(0, group, i).wait_send()
-
-        @pl.loop(1, nz)
-        def _(t):
-            facts_copy(lax.rem(z + t, nz), z).wait_send()
+        sent(x_send.at[pl.ds(0, ns - 1)], x_sem.at[0])
+        sent(e_send.at[pl.ds(0, ns - 1)], e_sem.at[0])
+        sent(d_recv.at[pl.ds(0, ns - 1)], d_sem.at[0])
+        sent(z_send.at[pl.ds(0, nz - 1)], z_sem.at[0])
 
     def s_done():
-        @pl.loop(1, nz)
-        def _(t):
-            for u in range(2):
-                for part in range(2):
-                    over_z(s_send, s_recv, s_ss, s_rs, u, part, lax.rem(z + t, nz), z).wait_send()
+        sent(s_send.at[:, pl.ds(0, nz - 1)], s_ss.at[0])
 
     def fin_copy(slot):
         return pltpu.make_async_remote_copy(
@@ -380,23 +354,23 @@
     other_rows = pl.ds(pl.multiple_of(other * ROWS, ROWS), ROWS)
 
     def out_own(b):
-        return pltpu.make_async_copy(out.at[b, mine_rows], att_ref.at[:, columns(b, core)], o_own.at[b])
+        return pltpu.make_async_copy(out.at[b, mine_rows], att_ref.at[:, columns(b, core)], o_sem.at[0])
 
     def out_swap(b):
-        return to_partner(out.at[b, other_rows], att_ref.at[:, columns(b, core)], o_ss.at[b], o_rs.at[b])
-
-    def out_arrival(b):
-        return to_partner(out.at[b, other_rows], att_ref.at[:, columns(b, other)], o_ss.at[b], o_rs.at[b])
+        return to_partner(out.at[b, other_rows], att_ref.at[:, columns(b, core)], o_sem.at[1], o_sem.at[2])
 
     def output(u):
+        for part in range(2 - u):
+            arrived(s_recv.at[u, pl.ds(0, nz - 1), part_rows[part]], s_rs.at[2 * u + part])
+
         @pl.loop(0, nz)
         def _(t):
             b = near(t)
 
-            @pl.when(t > 0)
-            def _():
-                for part in range(2):
-                    over_z(s_send, s_recv, s_ss, s_rs, u, part, b, b).wait_recv()
+            if u == 1:
+                @pl.when(t > 0)
+                def _():
+                    arrived(s_recv.at[u, b, part_rows[1]], s_rs.at[3 + b])
 
             carried = dot(rows_of(2, b, u), s_recv[u, b])
             mixed = within[2 * b + u] + carried * jnp.exp(run_all[2 * b + u])
@@ -417,11 +391,10 @@
     fin_copy(turn).wait_send()
     s_done()
 
-    @pl.loop(0, nz)
-    def _(b):
-        out_own(b).wait()
-        out_swap(b).wait_send()
-        out_arrival(b).wait_recv()
+    some = out.at[:, pl.ds(0, ROWS)]
+    pltpu.make_async_copy(some, some, o_sem.at[0]).wait()
+    sent(some, o_sem.at[1])
+    arrived(some, o_sem.at[2])
 
 
 def local(ns, nz, queries, keys, values, log_decay, cached_state, norm_gain):
@@ -449,7 +422,7 @@
             pltpu.VMEM((2 * nz, SPAN, HD), F32),
             pltpu.VMEM((2, nz, HD, HD), BF16),
             pltpu.VMEM((2, nz, HD, HD), BF16),
-            pltpu.VMEM((2, ns // 2, PIECE, HD), F32),
+            pltpu.VMEM((ns, PIECE, HD), F32),
             pltpu.VMEM((ns, PIECE, HD), F32),
             pltpu.VMEM((ns, PIECE, HD), F32),
             pltpu.VMEM((2, HD, HD), F32),
@@ -463,10 +436,9 @@
             pltpu.VMEM((nz, 8, HD), F32),
             pltpu.VMEM((2, PIECE, HD), F32),
             pltpu.VMEM((ns, PIECE, HD), F32),
-            dma((3,)), dma((3, nz)), dma((3, nz)), dma((2,)),
-            dma((2, 2, nz)), dma((2, 2, nz)), dma((2, ns // 2)), dma((ns,)), dma((ns,)), dma((2, ns // 2)),
-            dma((2, 2, nz)), dma((2, 2, nz)), dma((nz,)), dma((nz,)), dma((nz,)), dma((2,)), dma((3,)),
-            dma((nz,)), dma((nz,)), dma((ns,)), dma((ns,)),
+            dma((3,)), dma((1,)), dma((nz + 1,)), dma((2,)),
+            dma((1,)), dma((4,)), dma((2,)), dma((5,)), dma((1,)), dma((3 + nz,)),
+            dma((3,)), dma((2,)), dma((3,)), dma((2,)), dma((2,)),
         ],
         compiler_params=pltpu.CompilerParams(
             collective_id=0, has_side_effects=True, vmem_limit_bytes=60 * 1024 * 1024

time: 62.7 us -> 59 us (0.941)
  Pallas kernels: 59 us -> 55.3 us
    pallas_call x1, Pallas kernels: 59 us -> 55.3 us  [local(): pl.pallas_call(functools.partial(kernel, ns, nz), out_shape=(jax.ShapeDty...]
where the time goes in v3:
time: 59 us; the launch traced here: 58.8 us
  Pallas kernels  55.3 us (94%)
  local copies, waits for them, and re-layouts  2.88 us (5%)
  between operations  0.65 us (1%)
    pallas_call x1, Pallas kernels, local(): pl.pallas_call(functools.partial(kernel, ns, nz), out_shape=(jax.ShapeDty...  55.3 us
    unnamed x4, local copies, waits for them, and re-layouts  2.88 us

profile of v3, /device:TPU:1, one launch (start us, length us, event | category | flops | bytes accessed | tf_op | source)
XLA Modules:
  0.0 58.8 jit_solution(1806210899386659707)
XLA Ops:
  0.6 55.3 %shard_map.77 = (bf16[128,4096]{1,0:T(8,128)(2,1)}, f32[2,4,128]{2,1,0:T(4,128)}) custom-call(bf16[128,4096]{1,0:T(8,128)(2,1)} %q_ref.1, bf16[128,4096]{1,0:T(8,128)(2,1)} %k_ref.1, bf16[128,4096]{1,0:T(8,128)(2,1)} %v_ref.1, bf16[32,128]{1,0:T(8,128)(2,1)} %bitcast.1, f32[2,128,128]{2,1,0:T(8,128)} %cached_ref.1, f32[2,128]{1,0:T(2,128)} %gain_ref.1), custom_call_target="tpu_custom_call" | custom-call | flops 1000000000 | bytes 8388608 | tf_op jit(solution)/shard_map/pallas_call | solution.py:405
  55.9 0.0 copy-start
  55.9 2.3 %copy.10 = bf16[128,4096]{1,0:T(8,128)(2,1)} copy(bf16[128,4096]{1,0:T(8,128)(2,1)} %get-tuple-element.4) | data formatting | bytes 2097152
  58.2 0.0 copy-done
  58.2 0.6 %copy.11 = f32[2,4,128]{2,1,0:T(4,128)} copy(f32[2,4,128]{2,1,0:T(4,128)S(1)} %copy-done) | data formatting | bytes 8192
Async XLA Ops:
  55.9 2.3 %copy-start = (f32[2,4,128]{2,1,0:T(4,128)S(1)}, f32[2,4,128]{2,1,0:T(4,128)}, u32[]{:S(2)}) copy-start(f32[2,4,128]{2,1,0:T(4,128)} %get-tuple-element.5) | copy-start | bytes 12292

commit v4 on v3

--- a/solution.py
+++ b/solution.py
@@ -207,7 +207,8 @@
 
         send_part(u, 1)
         l_recv[u, z] = l_send[u, z]
-        if u == 0:
+
+        if u == 1:
             @pl.loop(0, nz)
             def _(t):
                 swap_copy(2, t).start()
@@ -244,7 +245,6 @@
             weights = (scores * jnp.exp(jnp.where(here, gap, NEVER))).astype(BF16)
             within[2 * b + u] = dot(weights, rows_of(1, b, u))
 
-    pl.loop(0, nz // 2)(inside)
 
     def column_sum(u, part):
         arrived(l_recv.at[u, pl.ds(0, nz - 1), part_rows[part]], l_rs.at[2 * u + part])
@@ -302,28 +302,29 @@
 
         def step(b, state):
             s_send[u, b, part_rows[part], :] = state.astype(BF16)
+
+            @pl.when(b != z)
+            def _():
+                over_z(s_send, s_recv, s_ss, s_rs, u, part, b, z, True).start()
+
             return jnp.exp(z_recv[b, u : u + 1, :]) * state + l_recv[u, b, part_rows[part], :].astype(F32)
 
         lax.fori_loop(0, nz, step, e_recv[u, HALF * part : HALF * (part + 1), :])
-
-        @pl.loop(0, nz - 1)
-        def _(t):
-            over_z(s_send, s_recv, s_ss, s_rs, u, part, order(t), z, True).start()
 
         if part == 1:
             s_recv[u, z] = s_send[u, z]
 
     column_sum(0, 0)
+    pl.loop(0 * nz // 8, 2 * nz // 8)(inside)
     column_sum(0, 1)
-    pl.loop(nz // 2, nz)(inside)
+    pl.loop(2 * nz // 8, 4 * nz // 8)(inside)
+    column_sum(1, 0)
     cached_own.wait()
-
     arrived(d_recv.at[pl.ds(0, ns - 1)], d_sem.at[1])
-
     columns_scan(0, 0)
-    column_sum(1, 0)
+    column_sum(1, 1)
     columns_scan(0, 1)
-    column_sum(1, 1)
+    pl.loop(4 * nz // 8, 8 * nz // 8)(inside)
     give(0, 0)
     columns_scan(1, 0)
     give(0, 1)
@@ -405,8 +406,8 @@
     return pl.pallas_call(
         functools.partial(kernel, ns, nz),
         out_shape=(
-            jax.ShapeDtypeStruct(queries.shape, BF16),
-            jax.ShapeDtypeStruct((2, HD // ns, HD), F32),
+            pltpu.VMEM(queries.shape, BF16),
+            pltpu.VMEM((2, HD // ns, HD), F32),
         ),
         in_specs=[anywhere] * 6,
         out_specs=(anywhere, vmem),
@@ -441,7 +442,7 @@
             dma((3,)), dma((2,)), dma((3,)), dma((2,)), dma((2,)),
         ],
         compiler_params=pltpu.CompilerParams(
-            collective_id=0, has_side_effects=True, vmem_limit_bytes=60 * 1024 * 1024
+            collective_id=0, has_side_effects=True, vmem_limit_bytes=58 * 1024 * 1024
         ),
         cost_estimate=pl.CostEstimate(flops=10**9, bytes_accessed=8 * 2**20, transcendentals=2 * 10**6),
     )(queries, keys, values, log_decay.T, cached_state, norm_gain)

time: 59 us -> 54.6 us (0.925)
  Pallas kernels: 55.3 us -> 52.3 us
  local copies, waits for them, and re-layouts: 2.88 us -> 1.56 us
    pallas_call x1, Pallas kernels: 55.3 us -> 52.3 us  [local(): pl.pallas_call(functools.partial(kernel, ns, nz), out_shape=(pltpu.VMEM(q...]
    unnamed x4 -> x2, local copies, waits for them, and re-layouts: 2.88 us -> 1.56 us
where the time goes in v4:
time: 54.6 us; the launch traced here: 54.5 us
  Pallas kernels  52.3 us (96%)
  local copies, waits for them, and re-layouts  1.56 us (3%)
  between operations  0.64 us (1%)
    pallas_call x1, Pallas kernels, local(): pl.pallas_call(functools.partial(kernel, ns, nz), out_shape=(pltpu.VMEM(q...  52.3 us
    unnamed x2, local copies, waits for them, and re-layouts  1.56 us

profile of v4, /device:TPU:1, one launch (start us, length us, event | category | flops | bytes accessed | tf_op | source)
XLA Modules:
  0.0 54.5 jit_solution(9265530588811761293)
XLA Ops:
  0.6 52.3 %shard_map.77 = (bf16[128,4096]{1,0:T(8,128)(2,1)S(1)}, f32[2,4,128]{2,1,0:T(4,128)S(1)}) custom-call(bf16[128,4096]{1,0:T(8,128)(2,1)} %q_ref.1, bf16[128,4096]{1,0:T(8,128)(2,1)} %k_ref.1, bf16[128,4096]{1,0:T(8,128)(2,1)} %v_ref.1, bf16[32,128]{1,0:T(8,128)(2,1)} %bitcast.1, f32[2,128,128]{2,1,0:T(8,128)} %cached_ref.1, f32[2,128]{1,0:T(2,128)} %gain_ref.1), custom_call_target="tpu_custom_call" | custom-call | flops 1000000000 | bytes 8388608 | tf_op jit(solution)/shard_map/pallas_call | solution.py:406
  52.9 1.0 %copy.10 = bf16[128,4096]{1,0:T(8,128)(2,1)} copy(bf16[128,4096]{1,0:T(8,128)(2,1)S(1)} %get-tuple-element.2) | data formatting | bytes 2097152
  53.9 0.6 %copy.11 = f32[2,4,128]{2,1,0:T(4,128)} copy(f32[2,4,128]{2,1,0:T(4,128)S(1)} %get-tuple-element.3) | data formatting | bytes 8192

commit v5 on v4

--- a/solution.py
+++ b/solution.py
@@ -201,18 +201,16 @@
             state = (both[:HD] + both[HD:]).astype(BF16)
             l_send[u, b] = state
 
-            @pl.when(t < nz - 1)
-            def _():
-                over_z(l_send, l_recv, l_ss, l_rs, u, 0, b, z).start()
-
-        send_part(u, 1)
+            if u == 0:
+                @pl.when(t < nz - 1)
+                def _():
+                    over_z(l_send, l_recv, l_ss, l_rs, u, 0, b, z).start()
+
+        if u == 0:
+            send_part(0, 1)
         l_recv[u, z] = l_send[u, z]
 
         if u == 1:
-            @pl.loop(0, nz)
-            def _(t):
-                swap_copy(2, t).start()
-
             arrived(z_recv.at[pl.ds(0, nz - 1)], z_sem.at[1])
             total = lax.fori_loop(0, nz, lambda b, sums: sums + z_recv[b], jnp.zeros((8, HD), F32))
             for v in range(2):
@@ -224,8 +222,14 @@
 
             d_recv[seq] = d_send[turn]
 
+            @pl.loop(0, nz)
+            def _(t):
+                swap_copy(2, t).start()
+
     def l_done():
         sent(l_send.at[:, pl.ds(0, nz - 1)], l_ss.at[0])
+
+    send_part(1, 0)
 
     own_copy(2).wait()
     arrived(tokens.at[2, other, :, halves], in_recv.at[nz])
@@ -252,11 +256,11 @@
         def add(b, sums):
             return jnp.exp(z_recv[b, u : u + 1, :]) * sums + l_recv[u, b, part_rows[part], :].astype(F32)
 
-        state = lax.fori_loop(0, nz, add, jnp.zeros((HALF, HD), F32))
+        state = lax.fori_loop(0, nz, add, jnp.zeros((HALF, HD), F32), unroll=True)
         for g in range(near_ns):
             x_send[2 * (near_ns * part + g) + u] = state[PIECE * g : PIECE * (g + 1)]
 
-        @pl.loop(0, near_ns)
+        @pl.loop(0, near_ns, unroll=True)
         def _(t):
             g = near_ns * part + lax.rem(group + 1 + t, near_ns)
 
@@ -278,13 +282,10 @@
                 piece = jnp.exp(d_recv[i]) * piece + x_recv[i]
             fin_all[u] = piece
 
-            @pl.loop(0, ns)
+            @pl.loop(0, ns - 1, unroll=True)
             def _(t):
-                i = lax.rem(seq + t + 3 * ns // 8, ns)
-
-                @pl.when(i != seq)
-                def _():
-                    entry_copy(u, group, i).start()
+                far = lax.rem(seq + 1 + lax.rem(t + 3 * ns // 8 - 1, ns - 1), ns)
+                entry_copy(u, group, far).start()
 
             e_recv[u, piece_rows(group), :] = e_send[seq]
 
@@ -309,12 +310,13 @@
 
             return jnp.exp(z_recv[b, u : u + 1, :]) * state + l_recv[u, b, part_rows[part], :].astype(F32)
 
-        lax.fori_loop(0, nz, step, e_recv[u, HALF * part : HALF * (part + 1), :])
+        lax.fori_loop(0, nz, step, e_recv[u, HALF * part : HALF * (part + 1), :], unroll=True)
 
         if part == 1:
             s_recv[u, z] = s_send[u, z]
 
     column_sum(0, 0)
+    send_part(1, 1)
     pl.loop(0 * nz // 8, 2 * nz // 8)(inside)
     column_sum(0, 1)
     pl.loop(2 * nz // 8, 4 * nz // 8)(inside)

time: 54.6 us -> 54.2 us (level)
  no operation moved by 1% of the time
where the time goes in v5:
time: 54.2 us; the launch traced here: 54.1 us
  Pallas kernels  51.9 us (96%)
  local copies, waits for them, and re-layouts  1.56 us (3%)
  between operations  0.64 us (1%)
    pallas_call x1, Pallas kernels, local(): pl.pallas_call(functools.partial(kernel, ns, nz), out_shape=(pltpu.VMEM(q...  51.9 us
    unnamed x2, local copies, waits for them, and re-layouts  1.56 us

profile of v5, /device:TPU:1, one launch (start us, length us, event | category | flops | bytes accessed | tf_op | source)
XLA Modules:
  0.0 54.1 jit_solution(12551936575353273149)
XLA Ops:
  0.6 51.9 %shard_map.77 = (bf16[128,4096]{1,0:T(8,128)(2,1)S(1)}, f32[2,4,128]{2,1,0:T(4,128)S(1)}) custom-call(bf16[128,4096]{1,0:T(8,128)(2,1)} %q_ref.1, bf16[128,4096]{1,0:T(8,128)(2,1)} %k_ref.1, bf16[128,4096]{1,0:T(8,128)(2,1)} %v_ref.1, bf16[32,128]{1,0:T(8,128)(2,1)} %bitcast.1, f32[2,128,128]{2,1,0:T(8,128)} %cached_ref.1, f32[2,128]{1,0:T(2,128)} %gain_ref.1), custom_call_target="tpu_custom_call" | custom-call | flops 1000000000 | bytes 8388608 | tf_op jit(solution)/shard_map/pallas_call | solution.py:408
  52.5 1.0 %copy.10 = bf16[128,4096]{1,0:T(8,128)(2,1)} copy(bf16[128,4096]{1,0:T(8,128)(2,1)S(1)} %get-tuple-element.2) | data formatting | bytes 2097152
  53.5 0.6 %copy.11 = f32[2,4,128]{2,1,0:T(4,128)} copy(f32[2,4,128]{2,1,0:T(4,128)S(1)} %get-tuple-element.3) | data formatting | bytes 8192
